TPU v7x, 128 devices: a whole 4x4x4 slice. The times are simulated.
128 devices in a mesh: freq: 32 (over x, y, core), dm: 4 (over z).
Axes of the slice: x: 4, y: 4, z: 4, core: 2. Of those that a mesh axis runs over, the one named last changes fastest.
Arguments:
- voltages: bfloat16 [2, 1024, 245760], P(None, ('freq', 'dm')), may hold values from -6 to 6
- filter_weights: float32 [4, 16384], replicated, may hold values from -3 to 3
- beam_delay_index: int32 [512, 1024], replicated, may hold values from 0 to 16383
- delays: int32 [256, 16384], P(None, ('freq', 'dm')), may hold values from 0 to 8
- dm_counts: int32 [128], replicated, may hold values from 1 to 4, 256 in all
Outputs:
- dedispersed: float32 [512, 4, 512], P(('freq', 'dm'))
Inputs may be any that keep to these rules, and one draw needn't show every extreme that they name: dm_counts sums to 256 and its largest entry is exactly 4.
All inputs are finite; a program needn't handle non-finite values.
Results may differ from a plain program's by a relative error of at most 0.0059.
Values may be sent and summed in bfloat16 or wider, within the bound.
A program may use at most 128 MiB of HBM per device.

v0:
```python
import math

import jax
import jax.numpy as jnp
from jax import lax
from jax.sharding import PartitionSpec as P

MAXD = 8
MOST_DM = 4


def rotation(in_count, out_count, period):
    row_ids = lax.iota(jnp.int32, in_count)[:, None]
    col_ids = lax.iota(jnp.int32, out_count)[None, :]
    phases = (row_ids * col_ids % period).astype(jnp.float32) * (2.0 * math.pi / period)
    return (jnp.cos(phases), jnp.sin(phases))


def fourier_transform(filter_output, inner):
    pair_value, batch, length = filter_output.shape
    outer = length // inner
    highest = lax.Precision.HIGHEST
    values = filter_output.reshape(2, batch, inner, outer)
    cos_first, sin_first = rotation(inner, inner, inner)
    by_cos = jnp.einsum("pbmn,mk->pbnk", values, cos_first, precision=highest)
    by_sin = jnp.einsum("pbmn,mk->pbnk", values, sin_first, precision=highest)
    part_re = by_cos[0] + by_sin[1]
    part_im = by_cos[1] - by_sin[0]
    cos_twist, sin_twist = rotation(outer, inner, length)
    twist_re = part_re * cos_twist + part_im * sin_twist
    twist_im = part_im * cos_twist - part_re * sin_twist
    twisted = jnp.stack([twist_re, twist_im])
    cos_second, sin_second = rotation(outer, outer, outer)
    by_cos = jnp.einsum("qn,pbnk->qpbk", cos_second, twisted, precision=highest)
    by_sin = jnp.einsum("qn,pbnk->qpbk", sin_second, twisted, precision=highest)
    out_re = by_cos[:, 0] + by_sin[:, 1]
    out_im = by_cos[:, 1] - by_sin[:, 0]
    return jnp.stack([out_re, out_im], 1) * length ** (-0.5)


def local(voltages, filter_weights, beam_delay_index, delays, dm_counts):
    pair_value, antenna_shard, sample_rows = voltages.shape
    tap_count, channel_number = filter_weights.shape
    spectrum_total = sample_rows // channel_number - tap_count + 1
    freq_size = lax.axis_size("freq")
    dm_size = lax.axis_size("dm")
    devices = freq_size * dm_size
    channel_shard = channel_number // devices
    inner = min(128, channel_shard)
    outer = channel_number // inner
    repeat = channel_shard // inner
    frame_rows = voltages.reshape(2, antenna_shard, sample_rows // channel_number, channel_number)
    filter_output = filter_weights[0] * frame_rows[:, :, 0:spectrum_total].astype(jnp.float32)
    for tap_number in range(1, tap_count):
        filter_output = filter_output + filter_weights[tap_number] * frame_rows[
            :, :, tap_number : tap_number + spectrum_total
        ].astype(jnp.float32)
    spectrum_rows = fourier_transform(
        filter_output.reshape(2, antenna_shard * spectrum_total, channel_number), inner
    ).astype(jnp.bfloat16)
    spectrum_rows = spectrum_rows.reshape(outer, 2, antenna_shard, spectrum_total, inner)
    turned = lax.all_to_all(spectrum_rows, ("freq", "dm"), split_axis=0, concat_axis=2, tiled=True)
    antennas = turned.shape[2]
    beams = beam_delay_index.shape[0]
    group_id = lax.axis_index("freq") * dm_size + lax.axis_index("dm")
    centre = group_id * channel_shard + channel_shard // 2
    phases = (beam_delay_index * centre % channel_number).astype(jnp.float32) * (
        2.0 * math.pi / channel_number
    )
    weight_real = jnp.cos(phases).astype(jnp.bfloat16)
    weight_imaginary = (-jnp.sin(phases)).astype(jnp.bfloat16)
    steering = jnp.concatenate(
        [
            jnp.concatenate([weight_real, -weight_imaginary], 1),
            jnp.concatenate([weight_imaginary, weight_real], 1),
        ],
        0,
    )
    steering = steering.reshape(2 * beams, 2, antennas)
    formed = jnp.einsum(
        "qpa,rpasi->qrsi", steering, turned, preferred_element_type=jnp.float32
    ) * antennas ** (-0.5)
    power = formed[:beams] * formed[:beams] + formed[beams:] * formed[beams:]
    centered = (power - jnp.mean(power, axis=2, keepdims=True)).astype(jnp.bfloat16)
    out_len = spectrum_total - MAXD
    shifted = jnp.stack([centered[:, :, lag : lag + out_len, :] for lag in range(MAXD + 1)])
    levels = lax.iota(jnp.int32, MAXD + 1)
    offsets = jnp.cumsum(dm_counts) - dm_counts
    scaling = channel_number ** (-0.5)
    slot_total = devices * MOST_DM
    slot_ids = lax.iota(jnp.int32, slot_total)
    owners = slot_ids // MOST_DM
    within = slot_ids % MOST_DM
    owner_match = owners[:, None] == lax.iota(jnp.int32, devices)[None, :]
    owner_offset = jnp.sum(jnp.where(owner_match, offsets[None, :], 0), axis=1)
    owner_count = jnp.sum(jnp.where(owner_match, dm_counts[None, :], 0), axis=1)
    trial_ids = jnp.clip(owner_offset + within, 0, delays.shape[0] - 1)
    present = within < owner_count
    delay_rows = jnp.take(delays, trial_ids, axis=0)
    slot_hot = ((delay_rows[:, None, :] == levels[None, :, None]) & present[:, None, None]).astype(
        jnp.bfloat16
    )
    onehot = slot_hot
    onehot = onehot.reshape(onehot.shape[0], MAXD + 1, repeat, inner)
    return lax.psum_scatter(
        jnp.einsum("jdri,dbrui->jub", onehot, shifted, preferred_element_type=jnp.float32)
        * scaling,
        ("freq", "dm"),
        scatter_dimension=0,
        tiled=True,
    )


def solution(mesh):
    in_specs = (P(None, ("freq", "dm"), None), P(), P(), P(None, ("freq", "dm")), P())
    out_specs = P(("freq", "dm"), None, None)
    return jax.shard_map(local, mesh=mesh, in_specs=in_specs, out_specs=out_specs, check_vma=False)
```

profile of v0, /device:TPU:1, one launch (start us, length us, event | category | flops | bytes accessed | tf_op | source)
XLA Modules:
  0.0 440.1 jit_solution(9196822871476793486)
XLA Ops:
  6.5 1.8 fusion.88
  8.4 15.3 %multiply_add_fusion = f32[2,8,12,16384]{3,1,2,0:T(8,128)} fusion(bf16[2,8,15,16384]{3,1,2,0:T(8,128)(2,1)} %bitcast.100, f32[16384]{0:T(1024)S(1)} %bitcast.106, f32[16384]{0:T(1024)S(1)} %bitcast.107, f32[16384]{0:T(1024)S(1)} %bitcast.105, f32[16384]{0:T(1024)S(1)} %bitcast.104), kind=kLoop, calls=%fused_computation.4 | loop fusion | flops 34603008 | bytes 38010880 | tf_op jit(solution)/shard_map/add | solution.py:55
  23.6 17.6 %copy.81 = f32[2,8,12,16384]{3,2,1,0:T(8,128)} copy(f32[2,8,12,16384]{3,1,2,0:T(8,128)} %multiply_add_fusion) | data formatting | bytes 25165824 | tf_op jit(solution)/shard_map/reshape;reshape | solution.py:23
  41.2 13.3 %reshape.209 = f32[2,96,128,128]{3,2,1,0:T(8,128)} reshape(f32[2,8,12,16384]{3,2,1,0:T(8,128)} %copy.81) | data formatting | bytes 25165824 | tf_op jit(solution)/shard_map/reshape;reshape | solution.py:23
  54.5 23.9 %fusion.40 = f32[2,96,128,128]{3,2,1,0:T(8,128)S(1)} fusion(f32[2,96,128,128]{3,2,1,0:T(8,128)} %reshape.209), kind=kOutput, calls=%fused_computation.74 | convolution fusion | flops 4832067584 | bytes 25165824 | tf_op jit(solution)/shard_map/pbmn,mk->pbnk/dot_general | solution.py:26
  78.3 23.7 %fusion.43 = f32[2,96,128,128]{3,2,1,0:T(8,128)} fusion(f32[2,96,128,128]{3,2,1,0:T(8,128)S(1)} %copy-done.1), kind=kOutput, calls=%fused_computation.77 | convolution fusion | flops 4832067584 | bytes 25165824 | tf_op jit(solution)/shard_map/pbmn,mk->pbnk/dot_general | solution.py:25
  102.4 8.1 %multiply_add_fusion.1 = (f32[1,96,128,128]{3,2,1,0:T(8,128)S(1)}, f32[1,96,128,128]{3,2,1,0:T(8,128)}) fusion(f32[128,128]{1,0:T(8,128)S(1)} %get-tuple-element.17, f32[128,128]{1,0:T(8,128)S(1)} %get-tuple-element.18, f32[2,96,128,128]{3,2,1,0:T(8,128)S(1)} %fusion.40, f32[2,96,128,128]{3,2,1,0:T(8,128)} %fusion.43), kind=kLoop, calls=%fused_computation.16 | loop fusion | flops 12582912 | bytes 37879808 | tf_op jit(solution)/shard_map/add | solution.py:30
  110.5 16.3 %fusion.2 = f32[128,2,96,128]{3,0,2,1:T(8,128)S(1)} fusion(f32[1,96,128,128]{3,2,1,0:T(8,128)} %get-tuple-element.10, f32[1,96,128,128]{3,2,1,0:T(8,128)S(1)} %get-tuple-element.9), kind=kOutput, calls=%fused_computation.6 | convolution fusion | flops 4835213312 | bytes 25165824 | tf_op jit(solution)/shard_map/qn,pbnk->qpbk/dot_general | solution.py:34
  126.8 14.7 %fusion.1 = f32[128,2,96,128]{3,0,2,1:T(8,128)} fusion(f32[1,96,128,128]{3,2,1,0:T(8,128)S(1)} %copy-done.2, f32[1,96,128,128]{3,2,1,0:T(8,128)S(1)} %get-tuple-element.9), kind=kOutput, calls=%fused_computation.5 | convolution fusion | flops 4835213312 | bytes 25165824 | tf_op jit(solution)/shard_map/qn,pbnk->qpbk/dot_general | solution.py:35
  141.5 7.6 %slice_add_fusion = (f32[128,1,96,128]{3,0,2,1:T(8,128)}, f32[128,1,96,128]{3,0,2,1:T(8,128)S(1)}) fusion(f32[128,2,96,128]{3,0,2,1:T(8,128)} %fusion.1, f32[128,2,96,128]{3,0,2,1:T(8,128)S(1)} %fusion.2), kind=kLoop, calls=%fused_computation.8 | loop fusion | flops 3145728 | bytes 37748736 | tf_op jit(solution)/shard_map/add | solution.py:36
  149.1 6.4 %copy.65 = f32[128,1,8,12,128]{4,2,3,1,0:T(8,128)S(1)} copy(f32[128,1,8,12,128]{4,0,3,2,1:T(8,128)} %bitcast.102) | data formatting | bytes 12582912 | tf_op jit(solution)/shard_map/stack | solution.py:38
  155.5 3.6 copy.66
  159.2 3.9 fusion
  163.1 11.9 %all-to-all-start = ((bf16[128,2,8,12,128]{4,2,3,1,0:T(8,128)(2,1)}), bf16[128,2,8,12,128]{4,2,3,1,0:T(8,128)(2,1)}, u32[]{:S(2)}, u32[]{:S(2)}) async-start(bf16[128,2,8,12,128]{4,2,3,1,0:T(8,128)(2,1)} %fusion), calls=%async_computation | async-start | bytes 12582912 | tf_op jit(solution)/shard_map/all_to_all | solution.py:62
  175.0 2.1 copy.61
  179.1 7.8 %cosine_convert_fusion = bf16[512,1024]{0,1:T(8,128)(2,1)S(1)} fusion(s32[512,1024]{0,1:T(8,128)S(1)} %copy.61, s32[]{:T(128)S(6)} %add.135), kind=kLoop, calls=%fused_computation.36 | loop fusion | flops 7864320 | bytes 3145732 | tf_op jit(solution)/shard_map/convert_element_type | solution.py:70
  186.9 8.1 %fusion.87 = (bf16[512,1024]{0,1:T(8,128)(2,1)S(1)}, bf16[512,1024]{0,1:T(8,128)(2,1)S(1)}) fusion(s32[512,1024]{0,1:T(8,128)S(1)} %copy.61, s32[]{:T(128)S(6)} %add.135), kind=kLoop, calls=%fused_computation.128 | loop fusion | flops 9961472 | bytes 4194308 | tf_op jit(solution)/shard_map/neg | solution.py:74
  195.0 17.8 %maximum_maximum_fusion = bf16[1024,2048]{0,1:T(8,128)(2,1)} fusion(bf16[512,1024]{0,1:T(8,128)(2,1)S(1)} %cosine_convert_fusion, bf16[512,1024]{0,1:T(8,128)(2,1)S(1)} %get-tuple-element.8, bf16[512,1024]{0,1:T(8,128)(2,1)S(1)} %get-tuple-element.7), kind=kLoop, calls=%fused_computation.19 | loop fusion | flops 16777216 | bytes 7340032 | tf_op jit(solution)/shard_map/concatenate | solution.py:72
  212.8 38.6 %all-to-all-done = bf16[128,2,8,12,128]{4,2,3,1,0:T(8,128)(2,1)} async-done(((bf16[128,2,8,12,128]{4,2,3,1,0:T(8,128)(2,1)}), bf16[128,2,8,12,128]{4,2,3,1,0:T(8,128)(2,1)}, u32[]{:S(2)}, u32[]{:S(2)}) %all-to-all-start) | async-done | bytes 6291488 | tf_op jit(solution)/shard_map/all_to_all | solution.py:62
  251.5 10.7 %bitcast_multiply_fusion = f32[1024,12,128]{2,0,1:T(8,128)S(1)} fusion(bf16[1024,2,1024,1]{0,2,1,3:T(8,128)(2,1)} %bitcast.103, bf16[128,2,8,12,128]{4,2,3,1,0:T(8,128)(2,1)} %all-to-all-done), kind=kOutput, calls=%fused_computation.11 | convolution fusion | flops 6444023808 | bytes 16777216 | tf_op jit(solution)/shard_map/qpa,rpasi->qrsi/dot_general | solution.py:80
  263.9 4.9 %fusion.8 = f32[512,4,512]{0,2,1:T(8,128)} fusion(bf16[9,512,1,4,128]{4,1,3,2,0:T(8,128)(2,1)S(1)} %fusion.26, s32[512,128]{1,0:T(8,128)S(1)} %broadcast_select_fusion, pred[512]{0:T(512)(128)(4,1)S(1)} %get-tuple-element.20), kind=kOutput, calls=%fused_computation.21 | convolution fusion | flops 2418147328 | bytes 9175552 | tf_op jit(solution)/shard_map/jdri,dbrui->jub/dot_general | solution.py:106
  268.8 5.4 %copy.70 = f32[512,4,512]{2,1,0:T(4,128)} copy(f32[512,4,512]{0,2,1:T(8,128)} %fusion.8) | data formatting | bytes 8388608 | tf_op jit(solution)/shard_map/mul | solution.py:106
  274.3 157.4 %all-reduce.3.cloned.1.call-done = f32[512,4,512]{2,1,0:T(4,128)} async-done(((f32[512,4,512]{2,1,0:T(4,128)}), f32[512,4,512]{2,1,0:T(4,128)}) %all-reduce.3.cloned.1.call-update) | async-done | bytes 4194320
  431.6 1.4 constant_dynamic-slice_fusion
  (34 shorter events, 3.9 us)
Async XLA Ops:
  6.5 171.4 %copy-start = (s32[256,128]{1,0:T(8,128)S(1)}, s32[256,128]{1,0:T(8,128)}, u32[]{:S(2)}) copy-start(s32[256,128]{1,0:T(8,128)} %param.8) | copy-start | bytes 393220
  54.5 23.9 %copy-start.1 = (f32[2,96,128,128]{3,2,1,0:T(8,128)S(1)}, f32[2,96,128,128]{3,2,1,0:T(8,128)}, u32[]{:S(2)}) copy-start(f32[2,96,128,128]{3,2,1,0:T(8,128)} %reshape.209) | copy-start | bytes 37748740
  110.5 16.3 %copy-start.2 = (f32[1,96,128,128]{3,2,1,0:T(8,128)S(1)}, f32[1,96,128,128]{3,2,1,0:T(8,128)}, u32[]{:S(2)}) copy-start(f32[1,96,128,128]{3,2,1,0:T(8,128)} %get-tuple-element.10) | copy-start | bytes 18874372
  163.1 14.1 %copy-start.3 = (s32[128]{0:T(128)S(1)}, s32[128]{0:T(128)}, u32[]{:S(2)}) copy-start(s32[128]{0:T(128)} %param.9) | copy-start | bytes 1540
  163.1 88.4 %all-to-all-start = ((bf16[128,2,8,12,128]{4,2,3,1,0:T(8,128)(2,1)}), bf16[128,2,8,12,128]{4,2,3,1,0:T(8,128)(2,1)}, u32[]{:S(2)}, u32[]{:S(2)}) async-start(bf16[128,2,8,12,128]{4,2,3,1,0:T(8,128)(2,1)} %fusion), calls=%async_computation | async-start | bytes 12582912 | tf_op jit(solution)/shard_map/all_to_all | solution.py:62
  175.0 256.7 %all-reduce.3.cloned.1.call-start = ((), (), s32[]{:S(2)}) async-start(), calls=%async_computation.1 | async-start | bytes 8388608
Sparse Core Ops, SparseCore 0:
  274.4 157.2 all-reduce.2
where the time goes:
time: 448 us; the launch traced here: 440 us
  waiting for transfers between devices  196 us (44%)
  matrix products  94.1 us (21%)
  other arithmetic  70.7 us (16%)
  local copies, waits for them, and re-layouts  53.4 us (12%)
  between operations  13.9 us (3%)
  starting transfers between devices  11.9 us (3%)
    unnamed x2, waiting for transfers between devices  157 us
    all_to_all x1, waiting for transfers between devices, local(): lax.all_to_all(spectrum_rows, ('freq', 'dm'), split_axis=0, concat_axis=2...  38.6 us
    another operation x2, local copies, waits for them, and re-layouts, fourier_transform(): values = filter_output.reshape(2, batch, inner, outer)  30.8 us
    dot_general x1, matrix products, fourier_transform(): by_sin = jnp.einsum('pbmn,mk->pbnk', values, sin_first, precision=highest)  23.9 us
    dot_general x1, matrix products, fourier_transform(): by_cos = jnp.einsum('pbmn,mk->pbnk', values, cos_first, precision=highest)  23.7 us
    concatenate x1, other arithmetic, local(): jnp.concatenate([jnp.concatenate([weight_real, -weight_imaginary], 1), jn...  17.8 us
    dot_general x1, matrix products, fourier_transform(): by_cos = jnp.einsum('qn,pbnk->qpbk', cos_second, twisted, precision=highest)  16.3 us
    add x1, other arithmetic, local(): filter_output + filter_weights[tap_number] * frame_rows[:, :, tap_number:...  15.3 us
  transfers between devices with their start and end apart: 2, of which 2 were waited for; matrix products, arithmetic and copies ran while one was open for 9% of the time, Pallas kernels for 0%

commit v1 on v0

v1 whole, which is shorter than its diff:
```python
import functools
import math

import jax
import jax.numpy as jnp
import ml_dtypes
import numpy as np
from jax import lax
from jax.experimental import pallas as pl
from jax.experimental.pallas import tpu as pltpu
from jax.sharding import PartitionSpec as P

MESH = pl.DeviceIdType.MESH
F32 = jnp.float32
BF16 = jnp.bfloat16

DEVICES = 128
CHIPS = 64
ANTENNAS = 8
SPECTRA = 12
TAPS = 4
FRAMES = SPECTRA + TAPS - 1
RADIX = 128
LENGTH = RADIX * RADIX
BEAMS = 512
TRIALS = 256
MOST_DM = 4
OUT_T = 4
GROUP = 2
ROWS = MOST_DM * OUT_T


def tables():
    ids = np.arange(RADIX)
    angle = 2.0 * np.pi * (np.outer(ids, ids) % RADIX) / RADIX
    dft = np.block([[np.cos(angle), np.sin(angle)], [-np.sin(angle), np.cos(angle)]])
    high = dft.astype(ml_dtypes.bfloat16)
    low = (dft - high.astype(np.float64)).astype(ml_dtypes.bfloat16)
    twist = 2.0 * np.pi * np.outer(ids, ids) / LENGTH
    scale = LENGTH**-0.5
    twist = np.concatenate([np.cos(twist) * scale, np.sin(twist) * scale]).astype(np.float32)
    return np.concatenate([high, high, low], axis=1), twist


def chip_orbits():
    far = lambda o: sum(min(v, 4 - v) for v in o)
    seen, orbits = set(), []
    for x in range(4):
        for y in range(4):
            for z in range(4):
                members = []
                for a, b, c in ((x, y, z), (y, z, x), (z, x, y)):
                    for sign in (1, -1):
                        member = (sign * a % 4, sign * b % 4, sign * c % 4)
                        if member not in members and member not in seen:
                            members.append(member)
                seen.update(members)
                if members:
                    orbits.append(members)
    orbits.sort(key=lambda m: -far(m[0]))
    return orbits


ORBITS = chip_orbits()
CHIP_ORDER = [o for m in ORBITS for o in m if o != (0, 0, 0)]
SEND_ORDER = [(o, c) for m in ORBITS for c in (0, 1) for o in m if (o, c) != ((0, 0, 0), 0)]


def position():
    freq, dm = lax.axis_index("freq"), lax.axis_index("dm")
    return freq // 8, (freq // 2) % 4, dm, freq % 2


def other(here, offset, core):
    x, y, z, c = here
    dx, dy, dz = offset
    return ((((x + dx) % 4) * 4 + (y + dy) % 4) * 2 + (c + core) % 2, (z + dz) % 4)


def index_of(device):
    return device[0] * 4 + device[1]


def halves(value):
    high = value.astype(BF16)
    return high, (value - high.astype(F32)).astype(BF16)


def body(
    volts, weights, beam_index, delays, counts, dft, twist, out,
    frames, taps, index, delay, count, dft_v, twist_v,
    filtered, first, second, turned_f32, sending, landed, steer, power, centered,
    hot, series, pair_send, pair_land, owner_send, owner_land,
    frame_sems, load_sems, own_sem, send_sem, land_sems, pair_sems, owner_sems,
):
    here = position()
    me = index_of((lax.axis_index("freq"), lax.axis_index("dm")))

    loads = [
        pltpu.make_async_copy(src, dst, load_sems.at[i])
        for i, (src, dst) in enumerate(
            [(weights, taps), (dft, dft_v), (twist, twist_v), (beam_index, index), (delays, delay), (counts, count)]
        )
    ]

    def frame_load(f):
        return pltpu.make_async_copy(
            volts.at[:, :, pl.ds(pl.multiple_of(f * LENGTH, LENGTH), LENGTH)], frames.at[f], frame_sems.at[f]
        )

    for f in range(TAPS):
        frame_load(f).start()
    for load in loads[:3]:
        load.start()
    for f in range(TAPS, FRAMES):
        frame_load(f).start()
    for load in loads[3:]:
        load.start()

    barrier = pltpu.get_barrier_semaphore()
    for offset, core in SEND_ORDER:
        pl.semaphore_signal(barrier, inc=1, device_id=other(here, offset, core), device_id_type=MESH)

    for load in loads[:3]:
        load.wait()
    for f in range(TAPS - 1):
        frame_load(f).wait()

    def channelize(s):
        frame_load(s + TAPS - 1).wait()
        wide = 1024

        def filter_part(part, _):
            at = pl.multiple_of(part * wide, wide)
            for p in range(2):
                total = taps[0:1, pl.ds(at, wide)] * frames[s, p, :, pl.ds(at, wide)].astype(F32)
                for k in range(1, TAPS):
                    total += taps[k : k + 1, pl.ds(at, wide)] * frames[s + k, p, :, pl.ds(at, wide)].astype(F32)
                for j in range(wide // RADIX):
                    row = p * RADIX * ANTENNAS + part * (wide // RADIX) * ANTENNAS + j * ANTENNAS
                    filtered[pl.ds(pl.multiple_of(row, ANTENNAS), ANTENNAS), :] = total[:, j * RADIX : (j + 1) * RADIX]
            return 0

        lax.fori_loop(0, LENGTH // wide, filter_part, 0)

        for pair in range(ANTENNAS // 2):
            for half in range(2):
                a = pair * 2 + half
                lanes = slice(half * RADIX, (half + 1) * RADIX)
                for p in range(2):
                    high, low = halves(filtered[pl.ds(p * RADIX * ANTENNAS + a, RADIX, stride=ANTENNAS), :])
                    first[pair, p * RADIX : (p + 1) * RADIX, lanes] = high
                    first[pair, (2 + p) * RADIX : (3 + p) * RADIX, lanes] = low
            part = jnp.dot(dft_v[:, 0:512], first[pair], preferred_element_type=F32)
            part += jnp.dot(dft_v[:, 512:768], first[pair, 0:256, :], preferred_element_type=F32)
            cos, sin = twist_v[0:RADIX, :], twist_v[RADIX:, :]
            for half in range(2):
                lanes = slice(half * RADIX, (half + 1) * RADIX)
                part_re, part_im = part[0:RADIX, lanes], part[RADIX:, lanes]
                for p, value in enumerate((part_re * cos + part_im * sin, part_im * cos - part_re * sin)):
                    high, low = halves(value)
                    rows = slice(half * RADIX, (half + 1) * RADIX)
                    second[pair, rows, p * RADIX : (p + 1) * RADIX] = high
                    second[pair, rows, (2 + p) * RADIX : (3 + p) * RADIX] = low
            contract = (((1,), (1,)), ((), ()))
            done = lax.dot_general(dft_v[:, 0:512], second[pair], contract, preferred_element_type=F32)
            done += lax.dot_general(dft_v[:, 512:768], second[pair, :, 0:256], contract, preferred_element_type=F32)
            for half in range(2):
                a = pair * 2 + half
                for p in range(2):
                    turned_f32[pl.ds(p * ANTENNAS + a, RADIX, stride=2 * ANTENNAS), :] = done[
                        p * RADIX : (p + 1) * RADIX, half * RADIX : (half + 1) * RADIX
                    ]
        sending[:, s] = turned_f32[...].reshape(DEVICES, 2 * ANTENNAS, RADIX).astype(BF16)

    def own_copy(group):
        span = pl.ds(group * GROUP, GROUP)
        return pltpu.make_async_copy(sending.at[me, span], landed.at[me, span], own_sem)

    def channelize_group(group, _):
        lax.fori_loop(0, GROUP, lambda i, _: (channelize(group * GROUP + i), 0)[1], 0)

        @pl.when(group == 0)
        def _():
            pl.semaphore_wait(barrier, DEVICES - 1)

        span = pl.ds(group * GROUP, GROUP)
        for offset, core in SEND_ORDER:
            device = other(here, offset, core)
            pltpu.make_async_remote_copy(
                src_ref=sending.at[index_of(device), span],
                dst_ref=landed.at[me, span],
                send_sem=send_sem,
                recv_sem=land_sems.at[group],
                device_id=device,
                device_id_type=MESH,
            ).start()
        copy = own_copy(group)
        copy.start()
        copy.wait()
        return 0

    lax.fori_loop(0, SPECTRA // GROUP, channelize_group, 0)

    loads[3].wait()
    centre = me * RADIX + RADIX // 2
    lane = lax.broadcasted_iota(jnp.int32, (RADIX, 256), 1)
    row = lax.broadcasted_iota(jnp.int32, (RADIX, 256), 0)
    spread = ((lane // 16) * 8 + lane % 8 == row).astype(F32).astype(BF16)
    quarter = ((lax.broadcasted_iota(jnp.int32, (64, 256), 1) // 8) % 2) * (LENGTH // 4)

    def steer_part(step, _):
        rows = pl.ds(pl.multiple_of((step // 8) * 64, 64), 64)
        block = step % 8
        found = index[rows, pl.ds(pl.multiple_of(block * RADIX, RADIX), RADIX)]
        high = (found >> 7).astype(F32).astype(BF16)
        low = (found & 127).astype(F32).astype(BF16)
        wide_high = jnp.dot(high, spread, preferred_element_type=F32)
        wide_low = jnp.dot(low, spread, preferred_element_type=F32)
        steps = (wide_high * 128.0 + wide_low).astype(jnp.int32)
        steps = (steps * centre - quarter) & (LENGTH - 1)
        turn = (steps + LENGTH // 8) >> 12
        x = (steps - (turn << 12)).astype(F32) * (2.0 * math.pi / LENGTH)
        y = x * x
        sin = x * (1.0 + y * (-1.0 / 6 + y * (1.0 / 120 + y * (-1.0 / 5040 + y * (1.0 / 362880)))))
        cos = 1.0 + y * (-0.5 + y * (1.0 / 24 + y * (-1.0 / 720 + y * (1.0 / 40320))))
        odd = (turn & 1) == 1
        cos_full = jnp.where(odd, sin, cos)
        sin_full = jnp.where(odd, cos, sin)
        cos_full = jnp.where(((turn + 1) & 2) == 2, -cos_full, cos_full)
        sin_full = jnp.where((turn & 2) == 2, -sin_full, sin_full)
        lanes = pl.ds(pl.multiple_of(block * 256, 256), 256)
        steer[rows, lanes] = cos_full.astype(BF16)
        steer[pl.ds(pl.multiple_of(BEAMS + (step // 8) * 64, 64), 64), lanes] = (-sin_full).astype(BF16)
        return 0

    lax.fori_loop(0, 64, steer_part, 0)

    loads[4].wait()
    loads[5].wait()
    more = (delay[...] + 1).astype(F32).astype(BF16)
    tally = count[...].astype(F32)
    x, y, z, c = here

    def hot_rows(block, owner):
        rows = lax.broadcasted_iota(jnp.int32, (ROWS, RADIX), 0)
        lanes = lax.broadcasted_iota(jnp.int32, (ROWS, RADIX), 1)
        before = jnp.sum(jnp.where(lanes < owner, tally, 0.0), axis=1, keepdims=True)
        mine = jnp.sum(jnp.where(lanes == owner, tally, 0.0), axis=1, keepdims=True)
        wide_rows = lax.broadcasted_iota(jnp.int32, (ROWS, TRIALS), 0)
        wide_lanes = lax.broadcasted_iota(jnp.int32, (ROWS, TRIALS), 1).astype(F32)
        within = (wide_rows // OUT_T).astype(F32)
        chosen = jnp.where((wide_lanes == before + within) & (within < mine), 1.0, 0.0).astype(BF16)
        level = jnp.dot(chosen, more, preferred_element_type=F32)
        level = jnp.where(level > 0.5, level + (rows % OUT_T).astype(F32) - 1.0, -1.0)
        for s in range(SPECTRA):
            hot[block * ROWS : (block + 1) * ROWS, s * RADIX : (s + 1) * RADIX] = jnp.where(
                level == float(s), 1.0, 0.0
            ).astype(BF16)

    for core in range(2):
        for i, offset in enumerate([(0, 0, 0)] + CHIP_ORDER):
            hot_rows(core * CHIPS + i, index_of(other(here, offset, core)))

    def beamform(group, _):
        span = pl.ds(group * GROUP, GROUP)
        arrived = landed.at[0 : DEVICES - 1, span]
        pltpu.make_async_copy(arrived, arrived, land_sems.at[group]).wait()
        spectra = jnp.concatenate(
            [landed[:, group * GROUP + i].reshape(DEVICES * 2 * ANTENNAS, RADIX) for i in range(GROUP)], axis=1
        )
        formed = jnp.dot(steer[...], spectra, preferred_element_type=F32)
        formed_re, formed_im = formed[:BEAMS], formed[BEAMS:]
        lanes = pl.ds(pl.multiple_of(group * GROUP * RADIX, GROUP * RADIX), GROUP * RADIX)
        power[:, lanes] = (formed_re * formed_re + formed_im * formed_im) * (1.0 / (DEVICES * ANTENNAS))
        return 0

    lax.fori_loop(0, SPECTRA // GROUP, beamform, 0)

    def centre_rows(step, _):
        rows = pl.ds(pl.multiple_of(step * 16, 16), 16)
        parts = [power[rows, s * RADIX : (s + 1) * RADIX] for s in range(SPECTRA)]
        mean = functools.reduce(lambda a, b: a + b, parts) * (1.0 / SPECTRA)
        for s, part in enumerate(parts):
            centered[rows, s * RADIX : (s + 1) * RADIX] = (part - mean).astype(BF16)
        return 0

    lax.fori_loop(0, BEAMS // 16, centre_rows, 0)

    contract = (((1,), (1,)), ((), ()))
    scale = LENGTH**-0.5
    half_rows = CHIPS * ROWS
    pair_send[...] = (
        lax.dot_general(hot[half_rows:, :], centered[...], contract, preferred_element_type=F32) * scale
    ).astype(BF16)
    pair = pltpu.make_async_remote_copy(
        src_ref=pair_send, dst_ref=pair_land, send_sem=pair_sems.at[0], recv_sem=pair_sems.at[1],
        device_id=other(here, (0, 0, 0), 1), device_id_type=MESH,
    )
    pair.start()
    series[...] = lax.dot_general(hot[0:half_rows, :], centered[...], contract, preferred_element_type=F32) * scale
    pair.wait()
    owner_send[...] = (series[ROWS:, :] + pair_land[ROWS:, :].astype(F32)).astype(BF16).reshape(CHIPS - 1, ROWS, BEAMS)
    for i, offset in enumerate(CHIP_ORDER):
        pltpu.make_async_remote_copy(
            src_ref=owner_send.at[i], dst_ref=owner_land.at[i], send_sem=owner_sems.at[0], recv_sem=owner_sems.at[1],
            device_id=other(here, offset, 0), device_id_type=MESH,
        ).start()
    total = series[0:ROWS, :] + pair_land[0:ROWS, :].astype(F32)
    pltpu.make_async_copy(owner_land, owner_land, owner_sems.at[1]).wait()
    total = lax.fori_loop(0, CHIPS - 1, lambda i, t: t + owner_land[i].astype(F32), total)
    for r in range(MOST_DM):
        out[r] = total[r * OUT_T : (r + 1) * OUT_T, :]

    pltpu.make_async_copy(owner_send, owner_send, owner_sems.at[0]).wait()
    gone = sending.at[0 : DEVICES - 1]
    pltpu.make_async_copy(gone, gone, send_sem).wait()


def local(voltages, filter_weights, beam_delay_index, delays, dm_counts):
    dft, twist = tables()
    anywhere = pl.BlockSpec(memory_space=pl.ANY)
    groups = SPECTRA // GROUP
    return pl.pallas_call(
        body,
        out_shape=jax.ShapeDtypeStruct((MOST_DM, OUT_T, BEAMS), F32),
        in_specs=[anywhere] * 7,
        out_specs=pl.BlockSpec(memory_space=pltpu.VMEM),
        scratch_shapes=[
            pltpu.VMEM((FRAMES, 2, ANTENNAS, LENGTH), BF16),
            pltpu.VMEM((TAPS, LENGTH), F32),
            pltpu.VMEM((BEAMS, DEVICES * ANTENNAS), jnp.int32),
            pltpu.VMEM((TRIALS, RADIX), jnp.int32),
            pltpu.VMEM((1, DEVICES), jnp.int32),
            pltpu.VMEM((256, 768), BF16),
            pltpu.VMEM((256, RADIX), F32),
            pltpu.VMEM((2 * RADIX * ANTENNAS, RADIX), F32),
            pltpu.VMEM((ANTENNAS // 2, 512, 256), BF16),
            pltpu.VMEM((ANTENNAS // 2, 256, 512), BF16),
            pltpu.VMEM((2 * RADIX * ANTENNAS, RADIX), F32),
            pltpu.VMEM((DEVICES, SPECTRA, 2 * ANTENNAS, RADIX), BF16),
            pltpu.VMEM((DEVICES, SPECTRA, 2 * ANTENNAS, RADIX), BF16),
            pltpu.VMEM((2 * BEAMS, DEVICES * 2 * ANTENNAS), BF16),
            pltpu.VMEM((BEAMS, SPECTRA * RADIX), F32),
            pltpu.VMEM((BEAMS, SPECTRA * RADIX), BF16),
            pltpu.VMEM((DEVICES * ROWS, SPECTRA * RADIX), BF16),
            pltpu.VMEM((CHIPS * ROWS, BEAMS), F32),
            pltpu.VMEM((CHIPS * ROWS, BEAMS), BF16),
            pltpu.VMEM((CHIPS * ROWS, BEAMS), BF16),
            pltpu.VMEM((CHIPS - 1, ROWS, BEAMS), BF16),
            pltpu.VMEM((CHIPS - 1, ROWS, BEAMS), BF16),
            pltpu.SemaphoreType.DMA((FRAMES,)),
            pltpu.SemaphoreType.DMA((6,)),
            pltpu.SemaphoreType.DMA,
            pltpu.SemaphoreType.DMA,
            pltpu.SemaphoreType.DMA((groups,)),
            pltpu.SemaphoreType.DMA((2,)),
            pltpu.SemaphoreType.DMA((2,)),
        ],
        compiler_params=pltpu.CompilerParams(
            collective_id=0, has_side_effects=True, vmem_limit_bytes=62 << 20
        ),
        cost_estimate=pl.CostEstimate(flops=16_000_000_000, bytes_accessed=12_000_000, transcendentals=0),
        name="channelize_turn_beamform",
    )(voltages, filter_weights, beam_delay_index, delays, dm_counts.reshape(1, DEVICES), dft, twist)


def solution(mesh):
    in_specs = (P(None, ("freq", "dm"), None), P(), P(), P(None, ("freq", "dm")), P())
    out_specs = P(("freq", "dm"), None, None)
    return jax.shard_map(local, mesh=mesh, in_specs=in_specs, out_specs=out_specs, check_vma=False)
```

time: 448 us -> 106 us (0.24); the launches traced: 440 us -> 106 us
  waiting for transfers between devices: 196 us -> 0 us
  Pallas kernels: 0 us -> 104 us
  matrix products: 94.1 us -> 0 us
  other arithmetic: 70.7 us -> 0 us
  local copies, waits for them, and re-layouts: 53.4 us -> 1.38 us
  between operations: 13.9 us -> 0.01 us
  starting transfers between devices: 11.9 us -> 0 us
    unnamed x2 -> x0, waiting for transfers between devices: 157 us -> none
    pallas_call x0 -> x1, Pallas kernels: none -> 104 us  [local(): pl.pallas_call(body, out_shape=jax.ShapeDtypeStruct((MOST_DM, OUT_T, BEAM...]
    dot_general x6 -> x0, matrix products: 94.1 us -> none  [the longest x1 23.9 us: fourier_transform(): by_sin = jnp.einsum('pbmn,mk->pbnk', values, sin_first, precision=highest)]
    another operation x6 -> x0, local copies, waits for them, and re-layouts: 41.1 us -> none  [the longest x2 30.8 us: fourier_transform(): values = filter_output.reshape(2, batch, inner, outer)]
    all_to_all x1 -> x0, waiting for transfers between devices: 38.6 us -> none  [local(): lax.all_to_all(spectrum_rows, ('freq', 'dm'), split_axis=0, concat_axis=2...]
    add x3 -> x0, other arithmetic: 31 us -> none  [the longest x1 15.3 us: local(): filter_output + filter_weights[tap_number] * frame_rows[:, :, tap_number:...]
    concatenate x1 -> x0, other arithmetic: 17.8 us -> none  [local(): jnp.concatenate([jnp.concatenate([weight_real, -weight_imaginary], 1), jn...]
    convert_element_type x3 -> x0, other arithmetic: 12.3 us -> none  [the longest x1 7.8 us: local(): weight_real = jnp.cos(phases).astype(jnp.bfloat16)]
  transfers between devices with their start and end apart: 2 -> 0, of which waited for: 2 -> 0; matrix products, arithmetic and copies ran while one was open for 9% -> 0% of each run, Pallas kernels for 0% -> 0%
where the time goes in v1:
time: 106 us
  Pallas kernels  104 us (98%)
  local copies, waits for them, and re-layouts  1.38 us (1%)
    pallas_call x1, Pallas kernels, local(): pl.pallas_call(body, out_shape=jax.ShapeDtypeStruct((MOST_DM, OUT_T, BEAM...  104 us

profile of v1, /device:TPU:1, one launch (start us, length us, event | category | flops | bytes accessed | tf_op | source)
XLA Modules:
  0.0 105.8 jit_solution(8113757788950117676)
XLA Ops:
  0.0 104.4 %channelize_turn_beamform.1 = f32[4,4,512]{2,1,0:T(4,128)} custom-call(bf16[2,8,245760]{2,1,0:T(8,128)(2,1)} %volts.1, f32[4,16384]{1,0:T(4,128)} %weights.1, s32[512,1024]{1,0:T(8,128)} %beam_index.1, s32[256,128]{1,0:T(8,128)} %delays.1, s32[1,128]{1,0:T(1,128)} %bitcast.1, bf16[256,768]{1,0:T(8,128)(2,1)} %constant.4.clone.dft, ...), custom_call_target="tpu_custom_call" | custom-call | flops 16000000000 | bytes 12000000 | tf_op jit(solution)/shard_map/channelize_turn_beamform/pallas_call | solution.py:324
  104.4 1.4 %copy.9 = f32[4,4,512]{2,1,0:T(4,128)} copy(f32[4,4,512]{2,1,0:T(4,128)} %channelize_turn_beamform.1) | data formatting | bytes 65536

commit v2 on v1

--- a/solution.py
+++ b/solution.py
@@ -27,6 +27,7 @@
 MOST_DM = 4
 OUT_T = 4
 GROUP = 2
+TILES = BEAMS // RADIX
 ROWS = MOST_DM * OUT_T
 
 
@@ -89,9 +90,9 @@
 def body(
     volts, weights, beam_index, delays, counts, dft, twist, out,
     frames, taps, index, delay, count, dft_v, twist_v,
-    filtered, first, second, turned_f32, sending, landed, steer, power, centered,
-    hot, series, pair_send, pair_land, owner_send, owner_land,
-    frame_sems, load_sems, own_sem, send_sem, land_sems, pair_sems, owner_sems,
+    filtered, first, second, turned_f32, sending, landed, steer, level_sum, level, centered,
+    hot, series, pair_send, pair_land, owner_own, owner_send, owner_land,
+    frame_sems, load_sems, send_sem, land_sems, pair_sems, owner_sems,
 ):
     here = position()
     me = index_of((lax.axis_index("freq"), lax.axis_index("dm")))
@@ -173,34 +174,27 @@
                     ]
         sending[:, s] = turned_f32[...].reshape(DEVICES, 2 * ANTENNAS, RADIX).astype(BF16)
 
-    def own_copy(group):
-        span = pl.ds(group * GROUP, GROUP)
-        return pltpu.make_async_copy(sending.at[me, span], landed.at[me, span], own_sem)
-
-    def channelize_group(group, _):
-        lax.fori_loop(0, GROUP, lambda i, _: (channelize(group * GROUP + i), 0)[1], 0)
-
-        @pl.when(group == 0)
+    def channelize_and_send(s, _):
+        channelize(s)
+
+        @pl.when(s == 0)
         def _():
             pl.semaphore_wait(barrier, DEVICES - 1)
 
-        span = pl.ds(group * GROUP, GROUP)
         for offset, core in SEND_ORDER:
             device = other(here, offset, core)
             pltpu.make_async_remote_copy(
-                src_ref=sending.at[index_of(device), span],
-                dst_ref=landed.at[me, span],
+                src_ref=sending.at[index_of(device), s],
+                dst_ref=landed.at[me, s],
                 send_sem=send_sem,
-                recv_sem=land_sems.at[group],
+                recv_sem=land_sems.at[s],
                 device_id=device,
                 device_id_type=MESH,
             ).start()
-        copy = own_copy(group)
-        copy.start()
-        copy.wait()
+        landed[me, s] = sending[me, s]
         return 0
 
-    lax.fori_loop(0, SPECTRA // GROUP, channelize_group, 0)
+    lax.fori_loop(0, SPECTRA, channelize_and_send, 0)
 
     loads[3].wait()
     centre = me * RADIX + RADIX // 2
@@ -242,6 +236,8 @@
     tally = count[...].astype(F32)
     x, y, z, c = here
 
+    scale = LENGTH**-0.5
+
     def hot_rows(block, owner):
         rows = lax.broadcasted_iota(jnp.int32, (ROWS, RADIX), 0)
         lanes = lax.broadcasted_iota(jnp.int32, (ROWS, RADIX), 1)
@@ -251,68 +247,98 @@
         wide_lanes = lax.broadcasted_iota(jnp.int32, (ROWS, TRIALS), 1).astype(F32)
         within = (wide_rows // OUT_T).astype(F32)
         chosen = jnp.where((wide_lanes == before + within) & (within < mine), 1.0, 0.0).astype(BF16)
-        level = jnp.dot(chosen, more, preferred_element_type=F32)
-        level = jnp.where(level > 0.5, level + (rows % OUT_T).astype(F32) - 1.0, -1.0)
+        late = jnp.dot(chosen, more, preferred_element_type=F32)
+        late = jnp.where(late > 0.5, late + (rows % OUT_T).astype(F32) - 1.0, -1.0)
         for s in range(SPECTRA):
             hot[block * ROWS : (block + 1) * ROWS, s * RADIX : (s + 1) * RADIX] = jnp.where(
-                level == float(s), 1.0, 0.0
+                late == float(s), scale, 0.0
             ).astype(BF16)
+        hot[block * ROWS : (block + 1) * ROWS, SPECTRA * RADIX :] = jnp.where(late >= 0.0, scale, 0.0).astype(BF16)
 
     for core in range(2):
         for i, offset in enumerate([(0, 0, 0)] + CHIP_ORDER):
             hot_rows(core * CHIPS + i, index_of(other(here, offset, core)))
 
+    contract = (((1,), (1,)), ((), ()))
+    half_rows = CHIPS * ROWS
+    block_rows = 256
+    level_sum[...] = jnp.zeros_like(level_sum)
+    level[...] = jnp.zeros_like(level)
+    series[...] = jnp.zeros_like(series)
+
     def beamform(group, _):
-        span = pl.ds(group * GROUP, GROUP)
-        arrived = landed.at[0 : DEVICES - 1, span]
-        pltpu.make_async_copy(arrived, arrived, land_sems.at[group]).wait()
+        for i in range(GROUP):
+            arrived = landed.at[0 : DEVICES - 1, group * GROUP + i]
+            pltpu.make_async_copy(arrived, arrived, land_sems.at[group * GROUP + i]).wait()
         spectra = jnp.concatenate(
             [landed[:, group * GROUP + i].reshape(DEVICES * 2 * ANTENNAS, RADIX) for i in range(GROUP)], axis=1
         )
         formed = jnp.dot(steer[...], spectra, preferred_element_type=F32)
         formed_re, formed_im = formed[:BEAMS], formed[BEAMS:]
-        lanes = pl.ds(pl.multiple_of(group * GROUP * RADIX, GROUP * RADIX), GROUP * RADIX)
-        power[:, lanes] = (formed_re * formed_re + formed_im * formed_im) * (1.0 / (DEVICES * ANTENNAS))
+        power = (formed_re * formed_re + formed_im * formed_im) * (1.0 / (DEVICES * ANTENNAS))
+        both = power[:, :RADIX] + power[:, RADIX:]
+        base = jnp.where(group == 0, both * (1.0 / GROUP), level[...])
+        level[...] = base
+        level_sum[...] += both
+        for i in range(GROUP):
+            at = pl.ds(pl.multiple_of((group * GROUP + i) * RADIX, RADIX), RADIX)
+            centered[:, at] = (power[:, i * RADIX : (i + 1) * RADIX] - base).astype(BF16)
+
+        @pl.when(group < SPECTRA // GROUP - 1)
+        def _():
+            at = pl.ds(pl.multiple_of(group * GROUP * RADIX, GROUP * RADIX), GROUP * RADIX)
+
+            def add_rows(step, _):
+                rows = pl.ds(pl.multiple_of(step * block_rows, block_rows), block_rows)
+                series[rows, :] += lax.dot_general(
+                    hot[rows, at], centered[:, at], contract, preferred_element_type=F32
+                )
+                return 0
+
+            lax.fori_loop(0, 2 * half_rows // block_rows, add_rows, 0)
+
         return 0
 
     lax.fori_loop(0, SPECTRA // GROUP, beamform, 0)
-
-    def centre_rows(step, _):
-        rows = pl.ds(pl.multiple_of(step * 16, 16), 16)
-        parts = [power[rows, s * RADIX : (s + 1) * RADIX] for s in range(SPECTRA)]
-        mean = functools.reduce(lambda a, b: a + b, parts) * (1.0 / SPECTRA)
-        for s, part in enumerate(parts):
-            centered[rows, s * RADIX : (s + 1) * RADIX] = (part - mean).astype(BF16)
-        return 0
-
-    lax.fori_loop(0, BEAMS // 16, centre_rows, 0)
-
-    contract = (((1,), (1,)), ((), ()))
-    scale = LENGTH**-0.5
-    half_rows = CHIPS * ROWS
-    pair_send[...] = (
-        lax.dot_general(hot[half_rows:, :], centered[...], contract, preferred_element_type=F32) * scale
-    ).astype(BF16)
-    pair = pltpu.make_async_remote_copy(
-        src_ref=pair_send, dst_ref=pair_land, send_sem=pair_sems.at[0], recv_sem=pair_sems.at[1],
-        device_id=other(here, (0, 0, 0), 1), device_id_type=MESH,
-    )
-    pair.start()
-    series[...] = lax.dot_general(hot[0:half_rows, :], centered[...], contract, preferred_element_type=F32) * scale
-    pair.wait()
-    owner_send[...] = (series[ROWS:, :] + pair_land[ROWS:, :].astype(F32)).astype(BF16).reshape(CHIPS - 1, ROWS, BEAMS)
-    for i, offset in enumerate(CHIP_ORDER):
-        pltpu.make_async_remote_copy(
-            src_ref=owner_send.at[i], dst_ref=owner_land.at[i], send_sem=owner_sems.at[0], recv_sem=owner_sems.at[1],
-            device_id=other(here, offset, 0), device_id_type=MESH,
-        ).start()
-    total = series[0:ROWS, :] + pair_land[0:ROWS, :].astype(F32)
-    pltpu.make_async_copy(owner_land, owner_land, owner_sems.at[1]).wait()
-    total = lax.fori_loop(0, CHIPS - 1, lambda i, t: t + owner_land[i].astype(F32), total)
-    for r in range(MOST_DM):
-        out[r] = total[r * OUT_T : (r + 1) * OUT_T, :]
-
-    pltpu.make_async_copy(owner_send, owner_send, owner_sems.at[0]).wait()
+    centered[:, SPECTRA * RADIX :] = (level[...] - level_sum[...] * (1.0 / SPECTRA)).astype(BF16)
+
+    def last_rows(rows, t):
+        at = slice((SPECTRA - GROUP) * RADIX, (SPECTRA + 1) * RADIX)
+        beams = slice(t * RADIX, (t + 1) * RADIX)
+        return series[rows, beams] + lax.dot_general(
+            hot[rows, at], centered[beams, at], contract, preferred_element_type=F32
+        )
+
+    def pair_copy(t):
+        return pltpu.make_async_remote_copy(
+            src_ref=pair_send.at[t], dst_ref=pair_land.at[t], send_sem=pair_sems.at[0, t], recv_sem=pair_sems.at[1, t],
+            device_id=other(here, (0, 0, 0), 1), device_id_type=MESH,
+        )
+
+    for t in range(TILES):
+        pair_send[t] = last_rows(slice(half_rows, 2 * half_rows), t).astype(BF16)
+        pair_copy(t).start()
+    for t in range(TILES):
+        mine = last_rows(slice(0, half_rows), t)
+        pair_copy(t).wait_recv()
+        mine += pair_land[t].astype(F32)
+        owner_own[t] = mine[0:ROWS, :]
+        owner_send[t] = mine[ROWS:, :].astype(BF16).reshape(CHIPS - 1, ROWS, RADIX)
+        for i, offset in enumerate(CHIP_ORDER):
+            pltpu.make_async_remote_copy(
+                src_ref=owner_send.at[t, i], dst_ref=owner_land.at[t, i],
+                send_sem=owner_sems.at[0, t], recv_sem=owner_sems.at[1, t],
+                device_id=other(here, offset, 0), device_id_type=MESH,
+            ).start()
+    for t in range(TILES):
+        pltpu.make_async_copy(owner_land.at[t], owner_land.at[t], owner_sems.at[1, t]).wait()
+        total = lax.fori_loop(0, CHIPS - 1, lambda i, total: total + owner_land[t, i].astype(F32), owner_own[t])
+        for r in range(MOST_DM):
+            out[r, :, t * RADIX : (t + 1) * RADIX] = total[r * OUT_T : (r + 1) * OUT_T, :]
+
+    for t in range(TILES):
+        pair_copy(t).wait_send()
+        pltpu.make_async_copy(owner_send.at[t], owner_send.at[t], owner_sems.at[0, t]).wait()
     gone = sending.at[0 : DEVICES - 1]
     pltpu.make_async_copy(gone, gone, send_sem).wait()
 
@@ -320,7 +346,6 @@
 def local(voltages, filter_weights, beam_delay_index, delays, dm_counts):
     dft, twist = tables()
     anywhere = pl.BlockSpec(memory_space=pl.ANY)
-    groups = SPECTRA // GROUP
     return pl.pallas_call(
         body,
         out_shape=jax.ShapeDtypeStruct((MOST_DM, OUT_T, BEAMS), F32),
@@ -341,21 +366,22 @@
             pltpu.VMEM((DEVICES, SPECTRA, 2 * ANTENNAS, RADIX), BF16),
             pltpu.VMEM((DEVICES, SPECTRA, 2 * ANTENNAS, RADIX), BF16),
             pltpu.VMEM((2 * BEAMS, DEVICES * 2 * ANTENNAS), BF16),
-            pltpu.VMEM((BEAMS, SPECTRA * RADIX), F32),
-            pltpu.VMEM((BEAMS, SPECTRA * RADIX), BF16),
-            pltpu.VMEM((DEVICES * ROWS, SPECTRA * RADIX), BF16),
-            pltpu.VMEM((CHIPS * ROWS, BEAMS), F32),
-            pltpu.VMEM((CHIPS * ROWS, BEAMS), BF16),
-            pltpu.VMEM((CHIPS * ROWS, BEAMS), BF16),
-            pltpu.VMEM((CHIPS - 1, ROWS, BEAMS), BF16),
-            pltpu.VMEM((CHIPS - 1, ROWS, BEAMS), BF16),
+            pltpu.VMEM((BEAMS, RADIX), F32),
+            pltpu.VMEM((BEAMS, RADIX), F32),
+            pltpu.VMEM((BEAMS, (SPECTRA + 1) * RADIX), BF16),
+            pltpu.VMEM((DEVICES * ROWS, (SPECTRA + 1) * RADIX), BF16),
+            pltpu.VMEM((DEVICES * ROWS, BEAMS), F32),
+            pltpu.VMEM((TILES, CHIPS * ROWS, RADIX), BF16),
+            pltpu.VMEM((TILES, CHIPS * ROWS, RADIX), BF16),
+            pltpu.VMEM((TILES, ROWS, RADIX), F32),
+            pltpu.VMEM((TILES, CHIPS - 1, ROWS, RADIX), BF16),
+            pltpu.VMEM((TILES, CHIPS - 1, ROWS, RADIX), BF16),
             pltpu.SemaphoreType.DMA((FRAMES,)),
             pltpu.SemaphoreType.DMA((6,)),
             pltpu.SemaphoreType.DMA,
-            pltpu.SemaphoreType.DMA,
-            pltpu.SemaphoreType.DMA((groups,)),
-            pltpu.SemaphoreType.DMA((2,)),
-            pltpu.SemaphoreType.DMA((2,)),
+            pltpu.SemaphoreType.DMA((SPECTRA,)),
+            pltpu.SemaphoreType.DMA((2, TILES)),
+            pltpu.SemaphoreType.DMA((2, TILES)),
         ],
         compiler_params=pltpu.CompilerParams(
             collective_id=0, has_side_effects=True, vmem_limit_bytes=62 << 20

time: 106 us -> 102 us (0.962)
  Pallas kernels: 104 us -> 100 us
    pallas_call x1, Pallas kernels: 104 us -> 100 us  [local(): pl.pallas_call(body, out_shape=jax.ShapeDtypeStruct((MOST_DM, OUT_T, BEAM...]
where the time goes in v2:
time: 102 us
  Pallas kernels  100 us (98%)
  local copies, waits for them, and re-layouts  1.38 us (1%)
    pallas_call x1, Pallas kernels, local(): pl.pallas_call(body, out_shape=jax.ShapeDtypeStruct((MOST_DM, OUT_T, BEAM...  100 us

profile of v2, /device:TPU:1, one launch (start us, length us, event | category | flops | bytes accessed | tf_op | source)
XLA Modules:
  0.0 101.8 jit_solution(11900699597897585658)
XLA Ops:
  0.0 100.5 %channelize_turn_beamform.1 = f32[4,4,512]{2,1,0:T(4,128)} custom-call(bf16[2,8,245760]{2,1,0:T(8,128)(2,1)} %volts.1, f32[4,16384]{1,0:T(4,128)} %weights.1, s32[512,1024]{1,0:T(8,128)} %beam_index.1, s32[256,128]{1,0:T(8,128)} %delays.1, s32[1,128]{1,0:T(1,128)} %bitcast.1, bf16[256,768]{1,0:T(8,128)(2,1)} %constant.4.clone.dft, ...), custom_call_target="tpu_custom_call" | custom-call | flops 16000000000 | bytes 12000000 | tf_op jit(solution)/shard_map/channelize_turn_beamform/pallas_call | solution.py:349
  100.5 1.4 %copy.9 = f32[4,4,512]{2,1,0:T(4,128)} copy(f32[4,4,512]{2,1,0:T(4,128)} %channelize_turn_beamform.1) | data formatting | bytes 65536

commit v3 on v2

--- a/solution.py
+++ b/solution.py
@@ -97,6 +97,10 @@
     here = position()
     me = index_of((lax.axis_index("freq"), lax.axis_index("dm")))
 
+    barrier = pltpu.get_barrier_semaphore()
+    for offset, core in SEND_ORDER:
+        pl.semaphore_signal(barrier, inc=1, device_id=other(here, offset, core), device_id_type=MESH)
+
     loads = [
         pltpu.make_async_copy(src, dst, load_sems.at[i])
         for i, (src, dst) in enumerate(
@@ -117,10 +121,6 @@
         frame_load(f).start()
     for load in loads[3:]:
         load.start()
-
-    barrier = pltpu.get_barrier_semaphore()
-    for offset, core in SEND_ORDER:
-        pl.semaphore_signal(barrier, inc=1, device_id=other(here, offset, core), device_id_type=MESH)
 
     for load in loads[:3]:
         load.wait()
@@ -266,16 +266,23 @@
     level[...] = jnp.zeros_like(level)
     series[...] = jnp.zeros_like(series)
 
-    def beamform(group, _):
+    def land(group):
         for i in range(GROUP):
             arrived = landed.at[0 : DEVICES - 1, group * GROUP + i]
             pltpu.make_async_copy(arrived, arrived, land_sems.at[group * GROUP + i]).wait()
-        spectra = jnp.concatenate(
+
+    def spectra_of(group):
+        return jnp.concatenate(
             [landed[:, group * GROUP + i].reshape(DEVICES * 2 * ANTENNAS, RADIX) for i in range(GROUP)], axis=1
         )
-        formed = jnp.dot(steer[...], spectra, preferred_element_type=F32)
-        formed_re, formed_im = formed[:BEAMS], formed[BEAMS:]
-        power = (formed_re * formed_re + formed_im * formed_im) * (1.0 / (DEVICES * ANTENNAS))
+
+    def power_of(formed_re, formed_im):
+        return (formed_re * formed_re + formed_im * formed_im) * (1.0 / (DEVICES * ANTENNAS))
+
+    def beamform(group, _):
+        land(group)
+        formed = jnp.dot(steer[...], spectra_of(group), preferred_element_type=F32)
+        power = power_of(formed[:BEAMS], formed[BEAMS:])
         both = power[:, :RADIX] + power[:, RADIX:]
         base = jnp.where(group == 0, both * (1.0 / GROUP), level[...])
         level[...] = base
@@ -283,27 +290,35 @@
         for i in range(GROUP):
             at = pl.ds(pl.multiple_of((group * GROUP + i) * RADIX, RADIX), RADIX)
             centered[:, at] = (power[:, i * RADIX : (i + 1) * RADIX] - base).astype(BF16)
-
-        @pl.when(group < SPECTRA // GROUP - 1)
-        def _():
-            at = pl.ds(pl.multiple_of(group * GROUP * RADIX, GROUP * RADIX), GROUP * RADIX)
-
-            def add_rows(step, _):
-                rows = pl.ds(pl.multiple_of(step * block_rows, block_rows), block_rows)
-                series[rows, :] += lax.dot_general(
-                    hot[rows, at], centered[:, at], contract, preferred_element_type=F32
-                )
-                return 0
-
-            lax.fori_loop(0, 2 * half_rows // block_rows, add_rows, 0)
-
+        at = pl.ds(pl.multiple_of(group * GROUP * RADIX, GROUP * RADIX), GROUP * RADIX)
+
+        def add_rows(step, _):
+            rows = pl.ds(pl.multiple_of(step * block_rows, block_rows), block_rows)
+            series[rows, :] += lax.dot_general(hot[rows, at], centered[:, at], contract, preferred_element_type=F32)
+            return 0
+
+        lax.fori_loop(0, 2 * half_rows // block_rows, add_rows, 0)
         return 0
 
-    lax.fori_loop(0, SPECTRA // GROUP, beamform, 0)
-    centered[:, SPECTRA * RADIX :] = (level[...] - level_sum[...] * (1.0 / SPECTRA)).astype(BF16)
+    last_group = SPECTRA // GROUP - 1
+    lax.fori_loop(0, last_group, beamform, 0)
+
+    def last_beams(t):
+        beams = slice(t * RADIX, (t + 1) * RADIX)
+        spectra = spectra_of(last_group)
+        power = power_of(
+            jnp.dot(steer[t * RADIX : (t + 1) * RADIX, :], spectra, preferred_element_type=F32),
+            jnp.dot(steer[BEAMS + t * RADIX : BEAMS + (t + 1) * RADIX, :], spectra, preferred_element_type=F32),
+        )
+        base = level[beams, :]
+        total = level_sum[beams, :] + power[:, :RADIX] + power[:, RADIX:]
+        for i in range(GROUP):
+            s = last_group * GROUP + i
+            centered[beams, s * RADIX : (s + 1) * RADIX] = (power[:, i * RADIX : (i + 1) * RADIX] - base).astype(BF16)
+        centered[beams, SPECTRA * RADIX :] = (base - total * (1.0 / SPECTRA)).astype(BF16)
 
     def last_rows(rows, t):
-        at = slice((SPECTRA - GROUP) * RADIX, (SPECTRA + 1) * RADIX)
+        at = slice(last_group * GROUP * RADIX, (SPECTRA + 1) * RADIX)
         beams = slice(t * RADIX, (t + 1) * RADIX)
         return series[rows, beams] + lax.dot_general(
             hot[rows, at], centered[beams, at], contract, preferred_element_type=F32
@@ -315,13 +330,9 @@
             device_id=other(here, (0, 0, 0), 1), device_id_type=MESH,
         )
 
-    for t in range(TILES):
-        pair_send[t] = last_rows(slice(half_rows, 2 * half_rows), t).astype(BF16)
-        pair_copy(t).start()
-    for t in range(TILES):
-        mine = last_rows(slice(0, half_rows), t)
+    def owners_out(t):
         pair_copy(t).wait_recv()
-        mine += pair_land[t].astype(F32)
+        mine = series[0:half_rows, t * RADIX : (t + 1) * RADIX] + pair_land[t].astype(F32)
         owner_own[t] = mine[0:ROWS, :]
         owner_send[t] = mine[ROWS:, :].astype(BF16).reshape(CHIPS - 1, ROWS, RADIX)
         for i, offset in enumerate(CHIP_ORDER):
@@ -330,9 +341,22 @@
                 send_sem=owner_sems.at[0, t], recv_sem=owner_sems.at[1, t],
                 device_id=other(here, offset, 0), device_id_type=MESH,
             ).start()
+
+    land(last_group)
+    for t in range(TILES):
+        last_beams(t)
+        pair_send[t] = last_rows(slice(half_rows, 2 * half_rows), t).astype(BF16)
+        pair_copy(t).start()
+        series[0:half_rows, t * RADIX : (t + 1) * RADIX] = last_rows(slice(0, half_rows), t)
+        if t > 0:
+            owners_out(t - 1)
+    owners_out(TILES - 1)
     for t in range(TILES):
         pltpu.make_async_copy(owner_land.at[t], owner_land.at[t], owner_sems.at[1, t]).wait()
-        total = lax.fori_loop(0, CHIPS - 1, lambda i, total: total + owner_land[t, i].astype(F32), owner_own[t])
+        totals = [owner_own[t], 0.0, 0.0, 0.0]
+        for i in range(CHIPS - 1):
+            totals[i % 4] += owner_land[t, i].astype(F32)
+        total = (totals[0] + totals[1]) + (totals[2] + totals[3])
         for r in range(MOST_DM):
             out[r, :, t * RADIX : (t + 1) * RADIX] = total[r * OUT_T : (r + 1) * OUT_T, :]
 

time: 102 us -> 102 us (level)
  no operation moved by 1% of the time
where the time goes in v3:
time: 102 us
  Pallas kernels  100 us (98%)
  local copies, waits for them, and re-layouts  1.38 us (1%)
    pallas_call x1, Pallas kernels, local(): pl.pallas_call(body, out_shape=jax.ShapeDtypeStruct((MOST_DM, OUT_T, BEAM...  100 us

profile of v3, /device:TPU:1, one launch (start us, length us, event | category | flops | bytes accessed | tf_op | source)
XLA Modules:
  0.0 101.5 jit_solution(6495241636505283395)
XLA Ops:
  0.0 100.1 %channelize_turn_beamform.1 = f32[4,4,512]{2,1,0:T(4,128)} custom-call(bf16[2,8,245760]{2,1,0:T(8,128)(2,1)} %volts.1, f32[4,16384]{1,0:T(4,128)} %weights.1, s32[512,1024]{1,0:T(8,128)} %beam_index.1, s32[256,128]{1,0:T(8,128)} %delays.1, s32[1,128]{1,0:T(1,128)} %bitcast.1, bf16[256,768]{1,0:T(8,128)(2,1)} %constant.4.clone.dft, ...), custom_call_target="tpu_custom_call" | custom-call | flops 16000000000 | bytes 12000000 | tf_op jit(solution)/shard_map/channelize_turn_beamform/pallas_call | solution.py:373
  100.1 1.4 %copy.9 = f32[4,4,512]{2,1,0:T(4,128)} copy(f32[4,4,512]{2,1,0:T(4,128)} %channelize_turn_beamform.1) | data formatting | bytes 65536

commit v4 on v3

--- a/solution.py
+++ b/solution.py
@@ -348,9 +348,7 @@
         pair_send[t] = last_rows(slice(half_rows, 2 * half_rows), t).astype(BF16)
         pair_copy(t).start()
         series[0:half_rows, t * RADIX : (t + 1) * RADIX] = last_rows(slice(0, half_rows), t)
-        if t > 0:
-            owners_out(t - 1)
-    owners_out(TILES - 1)
+        owners_out(t)
     for t in range(TILES):
         pltpu.make_async_copy(owner_land.at[t], owner_land.at[t], owner_sems.at[1, t]).wait()
         totals = [owner_own[t], 0.0, 0.0, 0.0]

time: 102 us -> 102 us (level)
  no operation moved by 1% of the time
where the time goes in v4:
time: 102 us
  Pallas kernels  100 us (98%)
  local copies, waits for them, and re-layouts  1.38 us (1%)
    pallas_call x1, Pallas kernels, local(): pl.pallas_call(body, out_shape=jax.ShapeDtypeStruct((MOST_DM, OUT_T, BEAM...  100 us

profile of v4, /device:TPU:1, one launch (start us, length us, event | category | flops | bytes accessed | tf_op | source)
XLA Modules:
  0.0 101.6 jit_solution(10017213376158527498)
XLA Ops:
  0.0 100.2 %channelize_turn_beamform.1 = f32[4,4,512]{2,1,0:T(4,128)} custom-call(bf16[2,8,245760]{2,1,0:T(8,128)(2,1)} %volts.1, f32[4,16384]{1,0:T(4,128)} %weights.1, s32[512,1024]{1,0:T(8,128)} %beam_index.1, s32[256,128]{1,0:T(8,128)} %delays.1, s32[1,128]{1,0:T(1,128)} %bitcast.1, bf16[256,768]{1,0:T(8,128)(2,1)} %constant.4.clone.dft, ...), custom_call_target="tpu_custom_call" | custom-call | flops 16000000000 | bytes 12000000 | tf_op jit(solution)/shard_map/channelize_turn_beamform/pallas_call | solution.py:371
  100.2 1.4 %copy.9 = f32[4,4,512]{2,1,0:T(4,128)} copy(f32[4,4,512]{2,1,0:T(4,128)} %channelize_turn_beamform.1) | data formatting | bytes 65536
